TPU v7x, 256 devices: a whole 4x4x8 slice. The times are simulated.
256 devices in a mesh: row: 8 (over z), col: 32 (over y, x, core).
Axes of the slice: x: 4, y: 4, z: 8, core: 2. Of those that a mesh axis runs over, the one named last changes fastest.
Arguments:
- states: bfloat16 [524288, 64], P(('row', 'col')), may hold values from -1.5 to 1.5
- right_sides: float32 [17, 524288], P(None, ('row', 'col')), may hold values from -120 to 120
- row_blocks: int32 [256, 320], P(('row', 'col')), may hold values from 0 to 511, as said below
- col_blocks: int32 [256, 320], P(('row', 'col')), may hold values from 0 to 127
- tile_counts: int32 [256], P(('row', 'col')), may hold values from 16 to 320, as said below
Outputs:
- solution: float32 [17, 524288], P(None, ('row', 'col'))
- residual: float32 [17, 524288], P(None, ('row', 'col'))
- direction: float32 [17, 524288], P(None, ('row', 'col'))
Inputs may be any that keep to these rules, and one draw needn't show every extreme that they name: `row_blocks`: the kept blocks fall into disjoint groups, and a tile is kept exactly when both of its blocks lie in one group. A device's blocks with local index below 16 / 2 (block g has local index g % 16) group only with blocks of devices of the same row index, and those with local index 8 or more only with blocks of devices of the same col index. Every kept unordered pair of blocks, a block with itself included, is named by exactly one live slot over all devices, in one of its two orders; the two blocks of a live tile lie on different devices unless the tile pairs a block with itself. The mirror (J, I) of a tile belongs to the device whose row index is that of block J's device and whose col index is that of block I's device; the live tiles of a device together with the mirrors of other devices' live tiles that belong to it number at most 320. Slots from tile_counts[d] on hold in-range numbers that name no tile.
All inputs are finite; a program needn't handle non-finite values.
Results may differ from a plain program's by a relative error of at most 0.0044.
Values may be sent and summed in bfloat16 or wider, within the bound.
A program may use at most 128 MiB of HBM per device.

v0:
```python
import math

import jax
import jax.numpy as jnp
from jax import lax
from jax.sharding import PartitionSpec as P

FEAT = 64
NV = 17
BLK = 128
SUB = 16


root_five = math.sqrt(5.0)
noise_level = 1.0
batch_tiles = 8


def matern(squared):
    scaled = root_five * jnp.sqrt(jnp.maximum(squared, 0.0))
    return (1.0 + scaled + scaled * scaled / 3.0) * jnp.exp(-scaled)


def squares_of(stacked):
    return jnp.sum(jnp.square(stacked.astype(jnp.float32)), axis=-1)


def tile_kernel(left_rows, right_rows, left_sq, right_sq):
    products = jnp.einsum("tak,tbk->tab", left_rows, right_rows, preferred_element_type=jnp.float32)
    return matern(left_sq[:, :, None] + right_sq[:, None, :] - 2.0 * products).astype(jnp.bfloat16)


def own_entries(row_blocks, col_blocks, tile_counts, row_index, col_index):
    rows_here = row_blocks[0]
    cols_here = col_blocks[0]
    diagonal = (
        (rows_here // SUB == col_index)
        & (cols_here // SUB == row_index)
        & (rows_here % SUB == cols_here % SUB)
    )
    return (rows_here, cols_here, diagonal.astype(jnp.int32), tile_counts[0])


def apply_tiles(entries, rows_x, cols_x, rows_vec, cols_vec):
    rows_sel, cols_sel, diag_sel, number = entries
    rows_sel = jnp.pad(rows_sel, (0, batch_tiles))
    cols_sel = jnp.pad(cols_sel, (0, batch_tiles))
    diag_sel = jnp.pad(diag_sel, (0, batch_tiles))
    row_stack = rows_x.reshape(-1, BLK, FEAT)
    col_stack = cols_x.reshape(-1, BLK, FEAT)
    row_sq = squares_of(row_stack)
    col_sq = squares_of(col_stack)
    col_vectors = cols_vec.reshape(NV, -1, BLK)
    row_vectors = rows_vec.reshape(NV, -1, BLK)
    initial = (
        jnp.zeros((NV, row_stack.shape[0], BLK), jnp.float32),
        jnp.zeros((NV, col_stack.shape[0], BLK), jnp.float32),
    )

    def advance(turn_index, totals):
        start_slot = turn_index * batch_tiles
        pick_rows = lax.dynamic_slice_in_dim(rows_sel, start_slot, batch_tiles)
        pick_cols = lax.dynamic_slice_in_dim(cols_sel, start_slot, batch_tiles)
        pick_diag = lax.dynamic_slice_in_dim(diag_sel, start_slot, batch_tiles)
        live_slots = start_slot + jnp.arange(batch_tiles, dtype=jnp.int32) < number
        kernel = tile_kernel(
            row_stack[pick_rows], col_stack[pick_cols], row_sq[pick_rows], col_sq[pick_cols]
        )
        kernel = kernel * live_slots.astype(jnp.bfloat16)[:, None, None]
        rowwise = jnp.einsum(
            "tab,vtb->vta", kernel, col_vectors[:, pick_cols], preferred_element_type=jnp.float32
        )
        mirror_weight = (1 - pick_diag).astype(jnp.float32)
        colwise = jnp.einsum(
            "tab,vta->vtb", kernel, row_vectors[:, pick_rows], preferred_element_type=jnp.float32
        )
        return (
            totals[0].at[:, pick_rows].add(rowwise),
            totals[1].at[:, pick_cols].add(colwise * mirror_weight[None, :, None]),
        )

    turn_total = (number + batch_tiles - 1) // batch_tiles
    return lax.fori_loop(jnp.int32(0), turn_total, advance, initial)


def shards(states, right_sides, row_blocks, col_blocks, tile_counts):
    row_index = lax.axis_index("row")
    col_index = lax.axis_index("col")
    vectors = right_sides.astype(jnp.bfloat16)
    entries = own_entries(row_blocks, col_blocks, tile_counts, row_index, col_index)
    rows_x, rows_vec = (
        lax.all_gather(states, "col", axis=0, tiled=True),
        lax.all_gather(vectors, "col", axis=1, tiled=True),
    )
    cols_x, cols_vec = (
        lax.all_gather(states, "row", axis=0, tiled=True),
        lax.all_gather(vectors, "row", axis=1, tiled=True),
    )
    totals = apply_tiles(entries, rows_x, cols_x, rows_vec, cols_vec)
    from_rows = lax.psum_scatter(totals[0].reshape(NV, -1), "col", scatter_dimension=1, tiled=True)
    from_cols = lax.psum_scatter(totals[1].reshape(NV, -1), "row", scatter_dimension=1, tiled=True)
    applied = from_rows + from_cols + noise_level * right_sides
    old_local = jnp.sum(jnp.square(right_sides), axis=1)
    curve_local = jnp.sum(right_sides * applied, axis=1)
    old_norm, curvature = lax.psum((old_local, curve_local), ("row", "col"))
    step_size = old_norm / curvature
    residual = right_sides - step_size[:, None] * applied
    new_norm = lax.psum(jnp.sum(jnp.square(residual), axis=1), ("row", "col"))
    solution = step_size[:, None] * right_sides
    direction = residual + (new_norm / old_norm)[:, None] * right_sides
    return (solution, residual, direction)


def solution(mesh):
    placed = (
        P(("row", "col"), None),
        P(None, ("row", "col")),
        P(("row", "col"), None),
        P(("row", "col"), None),
        P(("row", "col")),
    )
    return jax.shard_map(
        shards,
        mesh=mesh,
        in_specs=placed,
        out_specs=(P(None, ("row", "col")), P(None, ("row", "col")), P(None, ("row", "col"))),
        check_vma=False,
    )
```

profile of v0, /device:TPU:1, one launch (start us, length us, event | category | flops | bytes accessed | tf_op | source)
XLA Modules:
  0.0 1213.9 jit_solution(17527431347488593425)
XLA Ops:
  7.9 1.6 convert_element_type.25
  11.0 0.7 reduce.2
  12.4 27.3 %all_gather.12 = bf16[17,16384]{1,0:T(8,128)(2,1)S(1)} all-gather(bf16[17,2048]{1,0:T(8,128)(2,1)} %convert_element_type.25), channel_id=1, replica_groups=mesh['row'=8,'col'=32] {'row'}, dimensions={1}, use_global_device_ids=true | all-gather | bytes 626688 | tf_op jit(solution)/shard_map/all_gather | solution.py:97
  40.4 14.1 %all-gather.6.cloned.1.call-done = bf16[16384,64]{0,1:T(8,128)(2,1)} async-done(((bf16[2048,64]{0,1:T(8,128)(2,1)}), bf16[16384,64]{0,1:T(8,128)(2,1)}) %all-gather.6.cloned.1.call-update) | async-done | bytes 2097168 | tf_op jit(solution)/shard_map/all_gather | solution.py:96
  54.5 5.0 copy.25
  60.0 49.0 %all-gather.8.cloned.1.call-done = bf16[17,65536]{1,0:T(8,128)(2,1)} async-done(((bf16[17,2048]{1,0:T(8,128)(2,1)}), bf16[17,65536]{1,0:T(8,128)(2,1)}) %all-gather.8.cloned.1.call-update) | async-done | bytes 2228240 | tf_op jit(solution)/shard_map/all_gather | solution.py:93
  109.1 2.6 copy.33
  111.9 3.2 copy.27
  115.1 54.1 %all-gather.4.cloned.1.call-done = bf16[65536,64]{0,1:T(8,128)(2,1)} async-done(((bf16[2048,64]{0,1:T(8,128)(2,1)}), bf16[65536,64]{0,1:T(8,128)(2,1)}) %all-gather.4.cloned.1.call-update) | async-done | bytes 8388624 | tf_op jit(solution)/shard_map/all_gather | solution.py:92
  169.1 15.6 %copy.24 = bf16[65536,64]{1,0:T(8,128)(2,1)} copy(bf16[65536,64]{0,1:T(8,128)(2,1)} %all-gather.4.cloned.1.call-done) | data formatting | bytes 16777216 | tf_op jit(solution)/shard_map/all_gather | solution.py:92
  184.7 5.4 multiply_reduce_fusion
  190.1 3.1 broadcast_in_dim.8
  193.3 90.6 %while.12 = (s32[]{:T(128)}, f32[17,512,128]{2,0,1:T(8,128)}, f32[17,128,128]{2,0,1:T(8,128)S(1)}, s32[]{:T(128)}, s32[328]{0:T(512)S(1)}, /*index=5*/s32[328]{0...) while((s32[]{:T(128)}, f32[17,512,128]{2,0,1:T(8,128)}, ...), condition=%wide.region_7.8_spmd, body=%wide.region_4.7_spmd.sunk | while | flops 27448412 | bytes 2372387 | solution.py:83
  193.4 6.4 gather_fusion
  199.8 2.8 gather_fusion.1
  205.8 2.1 scatter_fusion
  207.9 2.5 gather_fusion.5
  210.6 0.8 scatter_fusion.1
  211.5 6.4 gather_fusion
  217.9 2.8 gather_fusion.1
  223.9 2.1 scatter_fusion
  226.0 2.5 gather_fusion.5
  228.7 0.8 scatter_fusion.1
  229.7 6.4 gather_fusion
  236.1 2.8 gather_fusion.1
  242.0 2.1 scatter_fusion
  244.1 2.5 gather_fusion.5
  246.9 0.8 scatter_fusion.1
  247.8 6.4 gather_fusion
  254.2 2.8 gather_fusion.1
  260.1 2.1 scatter_fusion
  262.3 2.5 gather_fusion.5
  265.0 0.8 scatter_fusion.1
  265.9 6.4 gather_fusion
  272.3 2.8 gather_fusion.1
  278.3 2.1 scatter_fusion
  280.4 2.5 gather_fusion.5
  283.1 0.8 scatter_fusion.1
  284.3 2.1 copy.35
  286.6 3.6 copy.28
  290.9 6.3 copy.34
  297.2 657.1 %reduce-scatter.5.cloned.1.call-done = f32[17,2048]{1,0:T(8,128)} async-done(((f32[17,16384]{1,0:T(8,128)}), f32[17,2048]{1,0:T(8,128)}) %reduce-scatter.5.cloned.1.call-update) | async-done | bytes 139280 | tf_op jit(solution)/shard_map/reduce_scatter | solution.py:101
  954.3 98.6 %reduce-scatter.3.cloned.1.call-done = f32[17,2048]{1,0:T(8,128)} async-done(((f32[17,65536]{1,0:T(8,128)}), f32[17,2048]{1,0:T(8,128)}) %reduce-scatter.3.cloned.1.call-update) | async-done | bytes 139280 | tf_op jit(solution)/shard_map/reduce_scatter | solution.py:100
  1052.9 1.2 multiply_reduce_fusion.3
  1054.1 77.2 %all-reduce.3 = (f32[17]{0:T(128)S(1)}, f32[17]{0:T(128)S(1)}) all-reduce(f32[17]{0:T(128)S(1)} %get-tuple-element.94, f32[17]{0:T(128)S(1)} %get-tuple-element.93), channel_id=1, replica_groups=mesh['row'=8,'col'=32] {'row','col'}, use_global_device_ids=true, to_apply=%region_1.2 | all-reduce | flops 34 | bytes 272 | tf_op jit(solution)/shard_map/psum | solution.py:105
  1131.3 1.9 multiply_reduce_fusion.2
  1133.3 73.3 %psum.23 = f32[17]{0:T(128)S(1)} all-reduce(f32[17]{0:T(128)S(1)} %get-tuple-element.125), channel_id=1, replica_groups=mesh['row'=8,'col'=32] {'row','col'}, use_global_device_ids=true, to_apply=%region_13.14 | all-reduce | flops 17 | bytes 136 | tf_op jit(solution)/shard_map/psum | solution.py:108
  1206.6 0.8 multiply_add_fusion
  (87 shorter events, 22.3 us)
Async XLA Ops:
  7.2 47.4 %all-gather.6.cloned.1.call-start = ((), (), s32[]{:S(2)}) async-start(), calls=%async_computation.3 | async-start | bytes 2359296 | tf_op jit(solution)/shard_map/all_gather | solution.py:96
  7.9 101.2 %all-gather.8.cloned.1.call-start = ((), (), s32[]{:S(2)}) async-start(), calls=%async_computation.4 | async-start | bytes 3244032 | tf_op jit(solution)/shard_map/all_gather | solution.py:93
  9.6 159.6 %all-gather.4.cloned.1.call-start = ((), (), s32[]{:S(2)}) async-start(), calls=%async_computation.2 | async-start | bytes 8650752 | tf_op jit(solution)/shard_map/all_gather | solution.py:92
  10.3 944.0 %reduce-scatter.5.cloned.1.call-start = ((), (), s32[]{:S(2)}) async-start(), calls=%async_computation.6 | async-start | bytes 1769472 | tf_op jit(solution)/shard_map/reduce_scatter | solution.py:101
  54.5 5.0 copy-start
  286.4 766.5 %reduce-scatter.3.cloned.1.call-start = ((), (), s32[]{:S(2)}) async-start(), calls=%async_computation.5 | async-start | bytes 6488064 | tf_op jit(solution)/shard_map/reduce_scatter | solution.py:100
  297.2 755.8 %copy-start.1 = (f32[17,2048]{1,0:T(8,128)S(1)}, f32[17,2048]{1,0:T(8,128)}, u32[]{:S(2)}) copy-start(f32[17,2048]{1,0:T(8,128)} %param.8) | copy-start | bytes 417796
  1133.3 74.1 %copy-start.2 = (f32[17,2048]{1,0:T(8,128)}, f32[17,2048]{1,0:T(8,128)S(1)}, u32[]{:S(2)}) copy-start(f32[17,2048]{1,0:T(8,128)S(1)} %get-tuple-element.126) | copy-start | bytes 417796
Sparse Core Ops, SparseCore 0:
  9.8 44.6 all-gather.5
  57.7 51.3 all-gather.7
  111.7 57.4 all-gather.3
  286.5 667.6 reduce-scatter.4
  958.1 94.7 reduce-scatter.2
where the time goes:
time: 1220 us; the launch traced here: 1210 us
  waiting for transfers between devices  874 us (72%)
  blocking collectives  178 us (15%)
  local copies, waits for them, and re-layouts  110 us (9%)
  other arithmetic  31.7 us (3%)
  between operations  14.6 us (1%)
    reduce_scatter x1, waiting for transfers between devices, shards(): lax.psum_scatter(totals[1].reshape(NV, -1), 'row', scatter_dimension=1, t...  657 us
    reduce_scatter x1, waiting for transfers between devices, shards(): lax.psum_scatter(totals[0].reshape(NV, -1), 'col', scatter_dimension=1, t...  98.6 us
    psum x1, blocking collectives, shards(): old_norm, curvature = lax.psum((old_local, curve_local), ('row', 'col'))  77.2 us
    psum x1, blocking collectives, shards(): new_norm = lax.psum(jnp.sum(jnp.square(residual), axis=1), ('row', 'col'))  73.3 us
    all_gather x1, waiting for transfers between devices, shards(): lax.all_gather(states, 'col', axis=0, tiled=True)  54.1 us
    all_gather x1, waiting for transfers between devices, shards(): lax.all_gather(vectors, 'col', axis=1, tiled=True)  49 us
    gather x5, local copies, waits for them, and re-layouts, advance(): row_stack[pick_rows]  31.8 us
    all_gather x1, blocking collectives, shards(): lax.all_gather(vectors, 'row', axis=1, tiled=True)  27.3 us
  transfers between devices with their start and end apart: 5, of which 5 were waited for; matrix products, arithmetic and copies ran while one was open for 2% of the time, Pallas kernels for 0%

commit v1 on v0

v1 whole, which is shorter than its diff:
```python
import math

import jax
import jax.numpy as jnp
from jax import lax
from jax.experimental import pallas as pl
from jax.experimental.pallas import tpu as pltpu
from jax.sharding import PartitionSpec as P

FEAT = 64
NV = 17
BLK = 128
HALF = 8
N_ROW = 8
N_COL = 32
MAXT = 320

V_AT, W_AT, E_AT, ROWS = 32, 40, 41, 45
PART_A, PART_B = (0, 22), (22, 45)
MESH = pl.DeviceIdType.MESH
NN = (((1,), (0,)), ((), ()))
NT = (((1,), (1,)), ((), ()))
rate = math.sqrt(5.0) * math.log2(math.e)
quad = math.log(2.0) ** 2 / 3.0
lin = math.log(2.0)


def dot(a, b, dims):
    return lax.dot_general(a, b, dims, preferred_element_type=jnp.float32)


def matern(squared):
    kept = jnp.maximum(squared, 1e-30)
    z = (kept * lax.rsqrt(kept)) * (-rate)
    return (((z * quad - lin) * z + 1.0) * jnp.exp2(z)).astype(jnp.bfloat16)


def split3(value):
    high = value.astype(jnp.bfloat16).astype(jnp.float32)
    rest = value - high
    middle = rest.astype(jnp.bfloat16).astype(jnp.float32)
    return high, middle, rest - middle


SOURCE_GROUPS = ((0,), (1, 3), (2,))
PLACE = {dx: (g, 2 * k) for g, group in enumerate(SOURCE_GROUPS) for k, dx in enumerate(group)}
SOURCES = [(dx, dk) for group in SOURCE_GROUPS for dx in group for dk in range(2)]


class Plan:
    def __init__(self):
        self.events = {}
        for m in (1, 3, 2):
            self.add("x%d" % m, "source", 0, (0, ROWS), m)
            self.add("y%d" % m, "output", 0, None, m)
            self.add("r%d" % m, "return", m, None, m)
        for dx in PLACE:
            self.add("s%d" % dx, "sibling", dx, (0, ROWS), 0)
        for step in range(4):
            for part, rows in (("a", PART_A), ("b", PART_B)):
                if step < 3 or part == "a":
                    self.add("u%d%s" % (step + 1, part), "stack", step, rows, 1)
                if step < 3 or part == "b":
                    self.add("d%d%s" % (step + 1, part), "stack", (8 - step) % 8, rows, 7)

    def add(self, name, *what):
        self.events[name] = (len(self.events),) + what


PLAN = Plan()
N_EVENT = len(PLAN.events)


def names(text):
    return text.split()


ROUND0 = names("s0 x1 x3 u1a") + names("d1a u1b d1b y1") + names("y3 x2 y2")
Z1 = [("u1a", "u2a"), ("d1a", "d2a"), ("u1b", "u2b"), ("d1b", "d2b")]
Z2 = [("u2a", "u3a"), ("d2a", "d3a"), ("u2b", "u3b"), ("d2b", "d3b")]
Z3 = [("u3a", "u4a"), ("d3b", "d4b"), ("u3b d3a", "")]


def kernel(
    count_ref, u_ref, v_ref, states_hbm, sides_hbm,
    applied_ref, coef_ref,
    states_ref, sides_ref, buf0, buf1, buf2, bufz, turned_ref, weights, mask_e, mask_v, acc, part_out, part_in,
    mine_ref, theirs_ref, wide_ref, prow, qrow, zrow, qall, ptab, ptab_smem, first_tab, first_smem,
    stat_out, stat1, stat2, stat2_out,
    ssem, rsem, tab_ssem, tab_rsem, st_ssem, st_rsem, local_sem,
):
    z = lax.axis_index("row")
    c = lax.axis_index("col")
    cy, cx, ck = c // 8, (c // 2) % 4, c % 2
    bufs = (buf0, buf1, buf2)
    spot = 2 * cx + ck
    load_states = pltpu.make_async_copy(states_hbm, states_ref, local_sem.at[0])
    load_sides = pltpu.make_async_copy(sides_hbm, sides_ref, local_sem.at[1])
    load_states.start()
    load_sides.start()

    def col_of(dx, dy, dk):
        other = (ck + 1) % 2 if dk else ck
        return (((cy + dy) % 4) * 4 + (cx + dx) % 4) * 2 + other

    barrier = pltpu.get_barrier_semaphore()

    def greet_col(o, carry):
        pl.semaphore_signal(barrier, inc=1, device_id=(z, (c + o) % N_COL), device_id_type=MESH)
        return carry

    def greet_row(o, carry):
        pl.semaphore_signal(barrier, inc=1, device_id=((z + o) % N_ROW, c), device_id_type=MESH)
        return carry

    lax.fori_loop(1, N_COL, greet_col, 0)
    lax.fori_loop(1, N_ROW, greet_row, 0)

    def copy(name):
        index, kind, slot, rows, move = PLAN.events[name]
        span = None if rows is None else pl.ds(rows[0], rows[1] - rows[0])
        if kind == "stack":
            src = bufz.at[slot, span]
            dst = bufz.at[(slot + move) % 8, span]
            target = ((z + move) % N_ROW, c)
        elif kind == "source":
            src = buf0.at[0, span]
            to_g, to_at = PLACE[move]
            dst = bufs[to_g].at[to_at, span]
            target = (z, col_of(move, 0, 0))
        elif kind == "sibling":
            g, at = PLACE[slot]
            src = bufs[g].at[at, span]
            dst = bufs[g].at[at + 1, span]
            target = (z, col_of(0, 0, 1))
        elif kind == "output":
            src = turned_ref.at[0]
            dst = turned_ref.at[move]
            target = (z, col_of(0, move, 0))
        else:
            src = part_out.at[slot - 1]
            dst = part_in.at[slot - 1]
            target = (z, col_of(0, -move, 0))
        return pltpu.make_async_remote_copy(
            src_ref=src, dst_ref=dst, send_sem=ssem.at[index], recv_sem=rsem.at[index],
            device_id=target, device_id_type=MESH,
        )

    def run(entries):
        for waits, starts in entries:
            for name in names(waits):
                copy(name).wait_recv()
            for name in names(starts):
                copy(name).start()

    t16 = lax.broadcasted_iota(jnp.int32, (16, 256), 0)
    n16 = lax.broadcasted_iota(jnp.int32, (16, 256), 1)
    ones16 = ((t16 < 3) & (n16 < 128)) | ((t16 >= 3) & (t16 < 6) & (n16 >= 128))
    ones16 = jnp.where(ones16, 1.0, 0.0).astype(jnp.bfloat16)
    row16 = lax.broadcasted_iota(jnp.int32, (16, 128), 0)
    load_states.wait()
    load_sides.wait()
    lane64 = lax.broadcasted_iota(jnp.int32, (64, 128), 1)
    for base, chunk in ((0, buf0), (HALF, bufz)):
        tail = jnp.where(lane64 % 16 // 3 == 2, 1.0, 0.0)
        for j in range(HALF):
            b = base + j
            turned = states_ref[:, b * BLK:(b + 1) * BLK].astype(jnp.float32)
            own_turned = turned_ref.at[0 if base == 0 else 4, j]
            own_turned[0:4] = (turned * -2.0).astype(jnp.bfloat16).reshape(4, 16, 128)
            small = jnp.zeros((16, 128), jnp.float32)
            for k, piece in enumerate(split3(jnp.sum(turned * turned, axis=0, keepdims=True))):
                small = jnp.where(row16 == 6 + k, piece, small)
            own_turned[4] = small.astype(jnp.bfloat16)
            block = turned.T
            feats = jnp.concatenate([block[:64], block[64:]], axis=1).astype(jnp.bfloat16)
            chunk[0, 4 * j:4 * j + 4] = feats.reshape(4, 16, 128)
            total = jnp.sum(block * block, axis=1, keepdims=True)
            for k, piece in enumerate(split3(total)):
                tail = jnp.where(lane64 == 16 * j + k, piece[:64], tail)
                tail = jnp.where(lane64 == 16 * j + 3 + k, piece[64:], tail)
            sides = sides_ref[:, b * BLK:(b + 1) * BLK]
            chunk[0, V_AT + j] = sides[:16].astype(jnp.bfloat16)
        last = [sides_ref[16:17, (base + j) * BLK:(base + j + 1) * BLK] for j in range(HALF)]
        last = jnp.concatenate(last + [jnp.zeros((8, 128), jnp.float32)], axis=0)
        chunk[0, W_AT] = last.astype(jnp.bfloat16)
        chunk[0, E_AT:E_AT + 4] = tail.astype(jnp.bfloat16).reshape(4, 16, 128)

    u, v = u_ref[...], v_ref[...]
    live = lax.broadcasted_iota(jnp.int32, (1, MAXT), 1) < count_ref[0]
    line = (u & 15) < HALF
    own = jnp.where(line, v & 15, (u & 15) - HALF)
    other = jnp.where(line, u & 15, (v & 15) - HALF)
    partner = jnp.where(live, jnp.where(line, u >> 4, N_COL + (v >> 4)), -1)
    hit = lax.broadcasted_iota(jnp.int32, (40, MAXT), 0) == partner
    lane40 = lax.broadcasted_iota(jnp.int32, (40, 128), 1)
    mine = jnp.zeros((40, 128), jnp.int32)
    theirs = jnp.zeros((40, 128), jnp.int32)
    for i in range(HALF):
        here = jnp.sum(jnp.where(hit & (own == i), other + 1, 0), axis=1, keepdims=True)
        there = jnp.sum(jnp.where(hit & (other == i), own + 1, 0), axis=1, keepdims=True)
        mine = jnp.where(lane40 == i, here, mine)
        theirs = jnp.where(lane40 == i, there, theirs)
    mine_ref[...] = mine
    theirs_ref[...] = theirs[N_COL:]
    wide = theirs[0:8]
    for y in range(1, 4):
        wide = wide + pltpu.roll(theirs[8 * y:8 * y + 8], 8 * y, 1)
    wide_ref[...] = wide
    qrow[spot] = wide
    zrow[z] = theirs[N_COL:]
    prow[0] = mine_ref[pl.ds(pl.multiple_of(8 * cy, 8), 8), :]

    pl.semaphore_wait(barrier, N_COL + N_ROW - 2)

    def share(src_of, dst, ssems, rsems, do_col, do_row, method):
        def col_step(o, carry):
            to = (c + o) % N_COL
            d = pltpu.make_async_remote_copy(
                src_ref=src_of(to), dst_ref=dst.at[c], send_sem=ssems.at[o], recv_sem=rsems.at[o],
                device_id=(z, to), device_id_type=MESH)
            getattr(d, method)()
            return carry

        def row_step(o, carry):
            to = (z + o) % N_ROW
            d = pltpu.make_async_remote_copy(
                src_ref=src_of(do_row + to), dst_ref=dst.at[do_row + z], send_sem=ssems.at[N_COL + o],
                recv_sem=rsems.at[N_COL + o], device_id=(to, c), device_id_type=MESH)
            getattr(d, method)()
            return carry

        if do_col:
            lax.fori_loop(1, N_COL, col_step, 0)
        if do_row is not None:
            lax.fori_loop(1, N_ROW, row_step, 0)

    def table(kind, method):
        if kind == "y":
            moves = [(20 + m, m, 0, 0) for m in (1, 3, 2)]
        elif kind == "x":
            moves = [(2 * m + k, 0, m, k) for m in (1, 3, 2) for k in range(2)]
        elif kind == "sibling":
            moves = [(1, 0, 0, 1)]
        else:
            moves = []
            for o in (4, 3, 5, 2, 6, 1, 7):
                getattr(pltpu.make_async_remote_copy(
                    src_ref=theirs_ref, dst_ref=zrow.at[z], send_sem=tab_ssem.at[8 + o],
                    recv_sem=tab_rsem.at[8 + o], device_id=((z + o) % N_ROW, c),
                    device_id_type=MESH), method)()
        for index, my, mx, mk in moves:
            if kind == "y":
                src = mine_ref.at[pl.ds(pl.multiple_of(8 * ((cy + my) % 4), 8), 8)]
                dst = prow.at[my]
            else:
                src, dst = wide_ref, qrow.at[spot]
            getattr(pltpu.make_async_remote_copy(
                src_ref=src, dst_ref=dst, send_sem=tab_ssem.at[index], recv_sem=tab_rsem.at[index],
                device_id=(z, col_of(mx, my, mk)), device_id_type=MESH), method)()

    KINDS = ("sibling", "x", "y", "z")
    for kind in KINDS:
        table(kind, "start")
    for name in ROUND0:
        copy(name).start()

    zero64 = jnp.zeros((64, 128), jnp.bfloat16)

    def weigh(slot):
        for j in range(HALF):
            at = 8 * slot + j
            scaled = turned_ref[slot, j, 0:4].reshape(64, 128)
            weights[at, 0:64, :] = jnp.concatenate([scaled, zero64], axis=1)
            weights[at, 64:128, :] = jnp.concatenate([zero64, scaled], axis=1)
            strip = turned_ref[slot, j, 4]
            small = jnp.concatenate([strip, strip], axis=1) + ones16
            for k in range(HALF):
                weights[at, 128 + 16 * k:144 + 16 * k, :] = small

    weigh(0)
    weigh(4)
    lane16 = lax.broadcasted_iota(jnp.int32, (16, 128), 1)
    row32 = lax.broadcasted_iota(jnp.int32, (32, 128), 0)
    for p in range(HALF + 1):
        mask_e[p] = jnp.where(lane16 // 16 == p - 1, 1.0, 0.0).astype(jnp.bfloat16)
        keep = (row32 < 16) | (row32 == 16 + p - 1) if p else row32 < 0
        mask_v[p] = jnp.where(keep, 1.0, 0.0).astype(jnp.bfloat16)

    def pairs(dy):
        shift = (128 - 8 * ((cy + 4 - dy) % 4)) % 128
        return jnp.maximum(prow[dy], pltpu.roll(qall[...], shift, 1))

    def source_row(dx, dk):
        return 2 * ((cx + 4 - dx) % 4) + ((ck + 1) % 2 if dk else ck)

    def group(sources, base, tab, rows, put, inside):
        def one(i):
            right = weights[base + i]
            parts, sides = [], []
            for s in range(len(rows)):
                buf, slot = sources[s]
                p = tab[rows[s], i]
                at = jnp.maximum(p - 1, 0)
                chosen = mask_e[p]
                for k in range(4):
                    parts.append(jnp.concatenate([buf[slot, at * 4 + k], buf[slot, E_AT + k] * chosen], axis=1))
                sides.append(jnp.concatenate([buf[slot, V_AT + at], buf[slot, W_AT]], axis=0) * mask_v[p])
            tiles = matern(dot(jnp.concatenate(parts, axis=0), right, NN))
            stacked = [
                tiles[64 * s:64 * s + 64, 128 * h:128 * h + 128] for s in range(len(rows)) for h in range(2)
            ]
            out = dot(jnp.concatenate(sides, axis=1), jnp.concatenate(stacked, axis=0), NN)
            last = jnp.sum(out[16:24], axis=0, keepdims=True)
            put(i, jnp.concatenate([out[:16], jnp.broadcast_to(last, (8, 128))], axis=0))

        def body(turn, carry):
            for at, entries in inside.items():
                @pl.when(turn == at)
                def _():
                    run(entries)
            one(2 * turn)
            one(2 * turn + 1)
            return carry

        lax.fori_loop(0, HALF // 2, body, 0)

    def put_own(base, first):
        def put(i, out):
            if first:
                acc[base + i] = out
            else:
                acc[base + i] += out
        return put

    def put_part(dy):
        def put(i, out):
            part_out[dy - 1, i] = out
        return put

    def of_group(g):
        return [(bufs[g], at) for at in range(2 * len(SOURCE_GROUPS[g]))]

    def rows_of(g):
        return [source_row(dx, dk) for dx in SOURCE_GROUPS[g] for dk in range(2)]

    for row in range(8):
        qall[row:row + 1, :] = jnp.zeros((1, 128), jnp.int32)
    sibling_row = source_row(0, 1)
    table("sibling", "wait_recv")
    qall[pl.ds(spot, 1), :] = qrow[spot, pl.ds(spot, 1), :]
    qall[pl.ds(sibling_row, 1), :] = qrow[sibling_row, pl.ds(spot, 1), :]
    first_tab[...] = pairs(0)
    to_smem = pltpu.make_async_copy(first_tab, first_smem, local_sem.at[0])
    to_smem.start()
    to_smem.wait()
    run([("s0", "")])
    group(of_group(0), 0, first_smem, rows_of(0), put_own(0, True), {})

    for kind in ("x", "y", "z"):
        table(kind, "wait_recv")
    for row in range(8):
        qall[row:row + 1, :] = qrow[row, pl.ds(spot, 1), :]
    for dy in range(4):
        ptab[8 * dy:8 * dy + 8, :] = pairs(dy)
    for row in range(8):
        qall[row:row + 1, :] = zrow[row, pl.ds(z, 1), :]
    ptab[N_COL:, :] = jnp.maximum(mine_ref[N_COL:, :], qall[...])
    to_smem = pltpu.make_async_copy(ptab, ptab_smem, local_sem.at[0])
    to_smem.start()
    to_smem.wait()

    run([("x1", "s1"), ("x3", "s3")] + Z1 + [("s1 s3", "")])
    group(of_group(1), 0, ptab_smem, rows_of(1), put_own(0, False), {3: [("x2", "s2")]})
    run([("s2", "")])
    group(of_group(2), 0, ptab_smem, rows_of(2), put_own(0, False), {1: Z2})
    everything = of_group(0) + of_group(1) + of_group(2)
    all_rows = rows_of(0) + rows_of(1) + rows_of(2)
    for dy, inside in ((1, {}), (3, {0: Z3}), (2, {})):
        run([("y%d" % dy, "")])
        weigh(dy)
        group(everything, 8 * dy, ptab_smem, [8 * dy + row for row in all_rows], put_part(dy), inside)
        run([("", "r%d" % dy)])
    run([("u4a d4b", "")])
    stack_rows = [N_COL + (z + N_ROW - d) % N_ROW for d in range(N_ROW)]
    group([(bufz, d) for d in range(N_ROW)], 4 * HALF, ptab_smem, stack_rows, put_own(HALF, True), {})
    run([("r1 r3 r2", "")])

    old = jnp.zeros((NV, 128), jnp.float32)
    curve = jnp.zeros((NV, 128), jnp.float32)
    for b in range(2 * HALF):
        product = acc[b]
        if b < HALF:
            product = product + part_in[0, b] + part_in[1, b] + part_in[2, b]
        sides = sides_ref[:, b * BLK:(b + 1) * BLK]
        applied = sides + product[:NV]
        applied_ref[:, b * BLK:(b + 1) * BLK] = applied
        old += sides * sides
        curve += sides * applied
    old = jnp.sum(old, axis=1, keepdims=True)
    curve = jnp.sum(curve, axis=1, keepdims=True)
    centre = jnp.where(curve > 0.0, jnp.minimum(old / curve, 1.0), 1.0)
    n_sum = jnp.zeros((NV, 128), jnp.float32)
    d_sum = jnp.zeros((NV, 128), jnp.float32)
    q_sum = jnp.zeros((NV, 128), jnp.float32)
    for b in range(2 * HALF):
        applied = applied_ref[:, b * BLK:(b + 1) * BLK]
        left = sides_ref[:, b * BLK:(b + 1) * BLK] - centre * applied
        n_sum += left * left
        d_sum += left * applied
        q_sum += applied * applied
    columns = [old, curve] + [jnp.sum(s, axis=1, keepdims=True) for s in (n_sum, d_sum, q_sum)] + [centre]
    lane17 = lax.broadcasted_iota(jnp.int32, (NV, 128), 1)
    packed = jnp.zeros((NV, 128), jnp.float32)
    for k, column in enumerate(columns):
        packed = jnp.where(lane17 == k, column, packed)
    packed = jnp.concatenate([packed, jnp.zeros((128 - NV, 128), jnp.float32)], axis=0)
    mine_stats = packed.T[0:8]

    def merge(stats):
        total = jnp.sum(stats, axis=0)
        old, curve, q = total[0:1], total[1:2], total[4:5]
        ratio = old / curve
        centre = jnp.where(curve > 0.0, jnp.minimum(ratio, 1.0), 1.0)

        def moved(to):
            eps = to - stats[:, 5:6, :]
            n = stats[:, 2:3, :] - 2.0 * eps * stats[:, 3:4, :] + eps * eps * stats[:, 4:5, :]
            return jnp.sum(n, axis=0), jnp.sum(stats[:, 3:4, :] - eps * stats[:, 4:5, :], axis=0)

        return old, curve, q, ratio, centre, moved

    stat_out[...] = mine_stats
    stat1[c] = mine_stats
    share(lambda at: stat_out, stat1, st_ssem, st_rsem, True, None, "start")
    share(lambda at: stat_out, stat1, st_ssem, st_rsem, True, None, "wait_recv")
    old, curve, q, ratio, centre, moved = merge(stat1[...])
    n, d = moved(centre)
    row_stats = jnp.concatenate([old, curve, n, d, q, centre, old, old], axis=0)
    stat2_out[...] = row_stats
    stat2[z] = row_stats
    share(lambda at: stat2_out, stat2, st_ssem, st_rsem, False, 0, "start")
    share(lambda at: stat2_out, stat2, st_ssem, st_rsem, False, 0, "wait_recv")
    old, curve, q, ratio, centre, moved = merge(stat2[...])
    n, d = moved(ratio)
    pair = jnp.concatenate([ratio, n / old, jnp.zeros((126, 128), jnp.float32)], axis=0)
    coef_ref[...] = pair.T[0:24]

    for name in PLAN.events:
        copy(name).wait_send()
    for kind in KINDS:
        table(kind, "wait_send")
    share(lambda at: stat_out, stat1, st_ssem, st_rsem, True, None, "wait_send")
    share(lambda at: stat2_out, stat2, st_ssem, st_rsem, False, 0, "wait_send")


def iterate(states, right_sides, row_blocks, col_blocks, tile_counts):
    vmem = pl.BlockSpec(memory_space=pltpu.VMEM)
    hbm = pl.BlockSpec(memory_space=pltpu.HBM)
    sizes = [2 * len(group) for group in SOURCE_GROUPS] + [N_ROW]
    table = pltpu.VMEM((8, 128), jnp.int32)
    return pl.pallas_call(
        kernel,
        out_shape=(
            jax.ShapeDtypeStruct((NV, 2048), jnp.float32),
            jax.ShapeDtypeStruct((24, 128), jnp.float32),
        ),
        in_specs=[pl.BlockSpec(memory_space=pltpu.SMEM), vmem, vmem, hbm, hbm],
        out_specs=(vmem, vmem),
        scratch_shapes=[
            pltpu.VMEM((FEAT, 2048), jnp.bfloat16),
            pltpu.VMEM((NV, 2048), jnp.float32),
        ] + [pltpu.VMEM((n, ROWS, 16, 128), jnp.bfloat16) for n in sizes] + [
            pltpu.VMEM((5, HALF, 5, 16, 128), jnp.bfloat16),
            pltpu.VMEM((5 * HALF, 256, 256), jnp.bfloat16),
            pltpu.VMEM((HALF + 1, 16, 128), jnp.bfloat16),
            pltpu.VMEM((HALF + 1, 32, 128), jnp.bfloat16),
            pltpu.VMEM((2 * HALF, 24, 128), jnp.float32),
            pltpu.VMEM((3, HALF, 24, 128), jnp.float32),
            pltpu.VMEM((3, HALF, 24, 128), jnp.float32),
            pltpu.VMEM((40, 128), jnp.int32),
            table,
            table,
            pltpu.VMEM((4, 8, 128), jnp.int32),
            pltpu.VMEM((8, 8, 128), jnp.int32),
            pltpu.VMEM((8, 8, 128), jnp.int32),
            table,
            pltpu.VMEM((40, 128), jnp.int32),
            pltpu.SMEM((40, 128), jnp.int32),
            table,
            pltpu.SMEM((8, 128), jnp.int32),
            pltpu.VMEM((8, 128), jnp.float32),
            pltpu.VMEM((N_COL, 8, 128), jnp.float32),
            pltpu.VMEM((N_ROW, 8, 128), jnp.float32),
            pltpu.VMEM((8, 128), jnp.float32),
            pltpu.SemaphoreType.DMA((N_EVENT,)),
            pltpu.SemaphoreType.DMA((N_EVENT,)),
            pltpu.SemaphoreType.DMA((N_COL + N_ROW,)),
            pltpu.SemaphoreType.DMA((N_COL + N_ROW,)),
            pltpu.SemaphoreType.DMA((N_COL + N_ROW,)),
            pltpu.SemaphoreType.DMA((N_COL + N_ROW,)),
            pltpu.SemaphoreType.DMA((2,)),
        ],
        compiler_params=pltpu.CompilerParams(
            collective_id=0, has_side_effects=True, vmem_limit_bytes=40 * 1024 * 1024
        ),
        name="gather_apply_reduce",
    )(tile_counts, row_blocks, col_blocks, states.T, right_sides)


def shards(states, right_sides, row_blocks, col_blocks, tile_counts):
    applied, coef = iterate(states, right_sides, row_blocks, col_blocks, tile_counts)
    step_size, ratio = coef[:NV, 0:1], coef[:NV, 1:2]
    residual = right_sides - step_size * applied
    return (step_size * right_sides, residual, residual + ratio * right_sides)


def solution(mesh):
    placed = (
        P(("row", "col"), None),
        P(None, ("row", "col")),
        P(("row", "col"), None),
        P(("row", "col"), None),
        P(("row", "col")),
    )
    return jax.shard_map(
        shards,
        mesh=mesh,
        in_specs=placed,
        out_specs=(P(None, ("row", "col")), P(None, ("row", "col")), P(None, ("row", "col"))),
        check_vma=False,
    )
```

time: 1220 us -> 57.9 us (0.05)
  waiting for transfers between devices: 874 us -> 0 us
  blocking collectives: 178 us -> 0 us
  local copies, waits for them, and re-layouts: 110 us -> 2.05 us
  Pallas kernels: 0 us -> 53.4 us
  other arithmetic: 31.7 us -> 0.92 us
  between operations: 14.6 us -> 1.35 us
    reduce_scatter x2 -> x0, waiting for transfers between devices: 756 us -> none  [the longest x1 657 us: shards(): lax.psum_scatter(totals[1].reshape(NV, -1), 'row', scatter_dimension=1, t...]
    psum x2 -> x0, blocking collectives: 151 us -> none  [the longest x1 77.2 us: shards(): old_norm, curvature = lax.psum((old_local, curve_local), ('row', 'col'))]
    all_gather x3 -> x0, waiting for transfers between devices: 117 us -> none  [the longest x1 54.1 us: shards(): lax.all_gather(states, 'col', axis=0, tiled=True)]
    gather x30 -> x0, local copies, waits for them, and re-layouts: 66.4 us -> none  [the longest x5 31.8 us: advance(): row_stack[pick_rows]]
    pallas_call x0 -> x1, Pallas kernels: none -> 53.4 us  [iterate(): pl.pallas_call(kernel, out_shape=(jax.ShapeDtypeStruct((NV, 2048), jnp.fl...]
    all_gather x1 -> x0, blocking collectives: 27.3 us -> none  [shards(): lax.all_gather(vectors, 'row', axis=1, tiled=True)]
    all_gather x2 -> x0, local copies, waits for them, and re-layouts: 20.6 us -> none  [the longest x1 15.6 us: shards(): lax.all_gather(states, 'col', axis=0, tiled=True)]
    scatter-add x10 -> x0, other arithmetic: 14.7 us -> none  [the longest x5 10.6 us: advance(): totals[0].at[:, pick_rows].add(rowwise)]
  transfers between devices with their start and end apart: 5 -> 0, of which waited for: 5 -> 0; matrix products, arithmetic and copies ran while one was open for 2% -> 0% of each run, Pallas kernels for 0% -> 0%
where the time goes in v1:
time: 57.9 us; the launch traced here: 57.7 us
  Pallas kernels  53.4 us (92%)
  local copies, waits for them, and re-layouts  2.05 us (4%)
  between operations  1.35 us (2%)
  other arithmetic  0.92 us (2%)
    pallas_call x1, Pallas kernels, iterate(): pl.pallas_call(kernel, out_shape=(jax.ShapeDtypeStruct((NV, 2048), jnp.fl...  53.4 us
    unnamed x8, local copies, waits for them, and re-layouts  1.88 us

profile of v1, /device:TPU:1, one launch (start us, length us, event | category | flops | bytes accessed | tf_op | source)
XLA Modules:
  0.0 57.7 jit_solution(430579162165676983)
XLA Ops:
  0.6 0.0 copy-start.3
  0.6 0.0 copy-start.2
  1.3 0.0 copy-done.3
  1.3 0.0 copy-done.2
  1.3 0.0 copy-start
  1.3 0.9 %copy-done = f32[17,2048]{1,0:T(8,128)S(1)} copy-done((f32[17,2048]{1,0:T(8,128)S(1)}, f32[17,2048]{1,0:T(8,128)}, u32[]{:S(2)}) %copy-start) | copy-done | bytes 139288
  2.3 0.0 copy-start.1
  2.3 0.9 %copy-done.1 = bf16[2048,64]{0,1:T(8,128)(2,1)S(1)} copy-done((bf16[2048,64]{0,1:T(8,128)(2,1)S(1)}, bf16[2048,64]{0,1:T(8,128)(2,1)}, u32[]{:S(2)}) %copy-start.1) | copy-done | bytes 262168
  3.2 53.4 %gather_apply_reduce.1 = (f32[17,2048]{1,0:T(8,128)S(1)}, f32[24,128]{1,0:T(8,128)S(1)}) custom-call(s32[1]{0:T(128)S(6)} %copy.8.count_ref, s32[1,320]{1,0:T(1,128)S(1)} %copy-done.2, s32[1,320]{1,0:T(1,128)S(1)} %copy-done.3, bf16[64,2048]{1,0:T(8,128)(2,1)S(1)} %bitcast.1, f32[17,2048]{1,0:T(8,128)S(1)} %copy-done), custom_call_target="tpu_custom_call" | custom-call | tf_op jit(solution)/shard_map/gather_apply_reduce/pallas_call | solution.py:462
  56.6 0.2 slice_reduce_fusion
  56.8 0.9 %multiply_add_fusion = (f32[17,2048]{1,0:T(8,128)}, f32[17,2048]{1,0:T(8,128)}, f32[17,2048]{1,0:T(8,128)}) fusion(f32[17,2048]{1,0:T(8,128)S(1)} %copy-done, f32[17]{0:T(128)S(1)} %get-tuple-element.7, f32[17,2048]{1,0:T(8,128)S(1)} %get-tuple-element.6, f32[17]{0:T(128)S(1)} %get-tuple-element.8), kind=kLoop, calls=%fused_computation | loop fusion | flops 174080 | bytes 696456 | tf_op jit(solution)/shard_map/add | solution.py:515
Async XLA Ops:
  0.6 0.7 %copy-start.3 = (s32[1,320]{1,0:T(1,128)S(1)}, s32[1,320]{1,0:T(1,128)}, u32[]{:S(2)}) copy-start(s32[1,320]{1,0:T(1,128)} %v_ref.1) | copy-start | bytes 3844
  0.6 0.7 %copy-start.2 = (s32[1,320]{1,0:T(1,128)S(1)}, s32[1,320]{1,0:T(1,128)}, u32[]{:S(2)}) copy-start(s32[1,320]{1,0:T(1,128)} %u_ref.1) | copy-start | bytes 3844
  1.3 0.9 %copy-start = (f32[17,2048]{1,0:T(8,128)S(1)}, f32[17,2048]{1,0:T(8,128)}, u32[]{:S(2)}) copy-start(f32[17,2048]{1,0:T(8,128)} %sides_hbm.1) | copy-start | bytes 417796
  2.3 0.9 %copy-start.1 = (bf16[2048,64]{0,1:T(8,128)(2,1)S(1)}, bf16[2048,64]{0,1:T(8,128)(2,1)}, u32[]{:S(2)}) copy-start(bf16[2048,64]{0,1:T(8,128)(2,1)} %param.5) | copy-start | bytes 786436

commit v2 on v1

--- a/solution.py
+++ b/solution.py
@@ -18,6 +18,8 @@
 V_AT, W_AT, E_AT, ROWS = 32, 40, 41, 45
 PART_A, PART_B = (0, 22), (22, 45)
 MESH = pl.DeviceIdType.MESH
+COL_ORDER = [*range(16, 24), *range(8, 16), *range(1, 8), *range(24, 32)]
+ROW_ORDER = [4, 3, 5, 2, 6, 1, 7]
 NN = (((1,), (0,)), ((), ()))
 NT = (((1,), (1,)), ((), ()))
 rate = math.sqrt(5.0) * math.log2(math.e)
@@ -43,8 +45,9 @@
 
 
 SOURCE_GROUPS = ((0,), (1, 3), (2,))
+OUTPUTS = (0, 1, 3, 2)
+STACK = 4
 PLACE = {dx: (g, 2 * k) for g, group in enumerate(SOURCE_GROUPS) for k, dx in enumerate(group)}
-SOURCES = [(dx, dk) for group in SOURCE_GROUPS for dx in group for dk in range(2)]
 
 
 class Plan:
@@ -75,17 +78,17 @@
     return text.split()
 
 
-ROUND0 = names("s0 x1 x3 u1a") + names("d1a u1b d1b y1") + names("y3 x2 y2")
+ROUND0 = names("s0 x1 x3 y1") + names("y3 u1a d1a") + names("u1b d1b")
 Z1 = [("u1a", "u2a"), ("d1a", "d2a"), ("u1b", "u2b"), ("d1b", "d2b")]
 Z2 = [("u2a", "u3a"), ("d2a", "d3a"), ("u2b", "u3b"), ("d2b", "d3b")]
 Z3 = [("u3a", "u4a"), ("d3b", "d4b"), ("u3b d3a", "")]
 
 
 def kernel(
-    count_ref, u_ref, v_ref, states_hbm, sides_hbm,
+    count_ref, u_hbm, v_hbm, states_hbm, sides_hbm,
     applied_ref, coef_ref,
-    states_ref, sides_ref, buf0, buf1, buf2, bufz, turned_ref, weights, mask_e, mask_v, acc, part_out, part_in,
-    mine_ref, theirs_ref, wide_ref, prow, qrow, zrow, qall, ptab, ptab_smem, first_tab, first_smem,
+    u_ref, v_ref, states_ref, sides_ref, buf0, buf1, buf2, bufz, turned_ref, weights, mask_e, mask_v, acc, part_in,
+    mine_ref, theirs_ref, wide_ref, prow, qrow, zrow, qall, ptab, ptab_smem, first_tab, first_smem, last_tab, last_smem,
     stat_out, stat1, stat2, stat2_out,
     ssem, rsem, tab_ssem, tab_rsem, st_ssem, st_rsem, local_sem,
 ):
@@ -96,8 +99,12 @@
     spot = 2 * cx + ck
     load_states = pltpu.make_async_copy(states_hbm, states_ref, local_sem.at[0])
     load_sides = pltpu.make_async_copy(sides_hbm, sides_ref, local_sem.at[1])
+    load_u = pltpu.make_async_copy(u_hbm, u_ref, local_sem.at[2])
+    load_v = pltpu.make_async_copy(v_hbm, v_ref, local_sem.at[3])
     load_states.start()
     load_sides.start()
+    load_u.start()
+    load_v.start()
 
     def col_of(dx, dy, dk):
         other = (ck + 1) % 2 if dk else ck
@@ -135,11 +142,11 @@
             target = (z, col_of(0, 0, 1))
         elif kind == "output":
             src = turned_ref.at[0]
-            dst = turned_ref.at[move]
+            dst = turned_ref.at[OUTPUTS.index(move)]
             target = (z, col_of(0, move, 0))
         else:
-            src = part_out.at[slot - 1]
-            dst = part_in.at[slot - 1]
+            src = acc.at[pl.ds(8 * OUTPUTS.index(slot), 8)]
+            dst = part_in.at[OUTPUTS.index(slot) - 1]
             target = (z, col_of(0, -move, 0))
         return pltpu.make_async_remote_copy(
             src_ref=src, dst_ref=dst, send_sem=ssem.at[index], recv_sem=rsem.at[index],
@@ -166,7 +173,7 @@
         for j in range(HALF):
             b = base + j
             turned = states_ref[:, b * BLK:(b + 1) * BLK].astype(jnp.float32)
-            own_turned = turned_ref.at[0 if base == 0 else 4, j]
+            own_turned = turned_ref.at[0 if base == 0 else STACK, j]
             own_turned[0:4] = (turned * -2.0).astype(jnp.bfloat16).reshape(4, 16, 128)
             small = jnp.zeros((16, 128), jnp.float32)
             for k, piece in enumerate(split3(jnp.sum(turned * turned, axis=0, keepdims=True))):
@@ -186,6 +193,8 @@
         chunk[0, W_AT] = last.astype(jnp.bfloat16)
         chunk[0, E_AT:E_AT + 4] = tail.astype(jnp.bfloat16).reshape(4, 16, 128)
 
+    load_u.wait()
+    load_v.wait()
     u, v = u_ref[...], v_ref[...]
     live = lax.broadcasted_iota(jnp.int32, (1, MAXT), 1) < count_ref[0]
     line = (u & 15) < HALF
@@ -211,29 +220,40 @@
     zrow[z] = theirs[N_COL:]
     prow[0] = mine_ref[pl.ds(pl.multiple_of(8 * cy, 8), 8), :]
 
+    zero64 = jnp.zeros((64, 128), jnp.bfloat16)
+
+    def weigh(slot):
+        for j in range(HALF):
+            at = 8 * slot + j
+            scaled = turned_ref[slot, j, 0:4].reshape(64, 128)
+            weights[at, 0:64, :] = jnp.concatenate([scaled, zero64], axis=1)
+            weights[at, 64:128, :] = jnp.concatenate([zero64, scaled], axis=1)
+            strip = turned_ref[slot, j, 4]
+            small = jnp.concatenate([strip, strip], axis=1) + ones16
+            for k in range(HALF):
+                weights[at, 128 + 16 * k:144 + 16 * k, :] = small
+
+    weigh(0)
+    lane16 = lax.broadcasted_iota(jnp.int32, (16, 128), 1)
+    row32 = lax.broadcasted_iota(jnp.int32, (32, 128), 0)
+    for p in range(HALF + 1):
+        mask_e[p] = jnp.where(lane16 // 16 == p - 1, 1.0, 0.0).astype(jnp.bfloat16)
+        keep = (row32 < 16) | (row32 == 16 + p - 1) if p else row32 < 0
+        mask_v[p] = jnp.where(keep, 1.0, 0.0).astype(jnp.bfloat16)
+
     pl.semaphore_wait(barrier, N_COL + N_ROW - 2)
 
-    def share(src_of, dst, ssems, rsems, do_col, do_row, method):
-        def col_step(o, carry):
-            to = (c + o) % N_COL
+    def share(src, dst, along_col, method):
+        offsets = COL_ORDER if along_col else ROW_ORDER
+        for o in offsets:
+            if along_col:
+                to, slot, sem = (z, (c + o) % N_COL), c, o
+            else:
+                to, slot, sem = ((z + o) % N_ROW, c), z, N_COL + o
             d = pltpu.make_async_remote_copy(
-                src_ref=src_of(to), dst_ref=dst.at[c], send_sem=ssems.at[o], recv_sem=rsems.at[o],
-                device_id=(z, to), device_id_type=MESH)
+                src_ref=src, dst_ref=dst.at[slot], send_sem=st_ssem.at[sem], recv_sem=st_rsem.at[sem],
+                device_id=to, device_id_type=MESH)
             getattr(d, method)()
-            return carry
-
-        def row_step(o, carry):
-            to = (z + o) % N_ROW
-            d = pltpu.make_async_remote_copy(
-                src_ref=src_of(do_row + to), dst_ref=dst.at[do_row + z], send_sem=ssems.at[N_COL + o],
-                recv_sem=rsems.at[N_COL + o], device_id=(to, c), device_id_type=MESH)
-            getattr(d, method)()
-            return carry
-
-        if do_col:
-            lax.fori_loop(1, N_COL, col_step, 0)
-        if do_row is not None:
-            lax.fori_loop(1, N_ROW, row_step, 0)
 
     def table(kind, method):
         if kind == "y":
@@ -265,28 +285,6 @@
     for name in ROUND0:
         copy(name).start()
 
-    zero64 = jnp.zeros((64, 128), jnp.bfloat16)
-
-    def weigh(slot):
-        for j in range(HALF):
-            at = 8 * slot + j
-            scaled = turned_ref[slot, j, 0:4].reshape(64, 128)
-            weights[at, 0:64, :] = jnp.concatenate([scaled, zero64], axis=1)
-            weights[at, 64:128, :] = jnp.concatenate([zero64, scaled], axis=1)
-            strip = turned_ref[slot, j, 4]
-            small = jnp.concatenate([strip, strip], axis=1) + ones16
-            for k in range(HALF):
-                weights[at, 128 + 16 * k:144 + 16 * k, :] = small
-
-    weigh(0)
-    weigh(4)
-    lane16 = lax.broadcasted_iota(jnp.int32, (16, 128), 1)
-    row32 = lax.broadcasted_iota(jnp.int32, (32, 128), 0)
-    for p in range(HALF + 1):
-        mask_e[p] = jnp.where(lane16 // 16 == p - 1, 1.0, 0.0).astype(jnp.bfloat16)
-        keep = (row32 < 16) | (row32 == 16 + p - 1) if p else row32 < 0
-        mask_v[p] = jnp.where(keep, 1.0, 0.0).astype(jnp.bfloat16)
-
     def pairs(dy):
         shift = (128 - 8 * ((cy + 4 - dy) % 4)) % 128
         return jnp.maximum(prow[dy], pltpu.roll(qall[...], shift, 1))
@@ -294,13 +292,13 @@
     def source_row(dx, dk):
         return 2 * ((cx + 4 - dx) % 4) + ((ck + 1) % 2 if dk else ck)
 
-    def group(sources, base, tab, rows, put, inside):
+    def group(sources, tab, rows, base, outputs, add, unroll, inside):
         def one(i):
             right = weights[base + i]
+            first_row = 0 if base == STACK * HALF else base + i - i % HALF
             parts, sides = [], []
-            for s in range(len(rows)):
-                buf, slot = sources[s]
-                p = tab[rows[s], i]
+            for (buf, slot), row in zip(sources, rows):
+                p = tab[row + first_row, i % HALF]
                 at = jnp.maximum(p - 1, 0)
                 chosen = mask_e[p]
                 for k in range(4):
@@ -308,41 +306,31 @@
                 sides.append(jnp.concatenate([buf[slot, V_AT + at], buf[slot, W_AT]], axis=0) * mask_v[p])
             tiles = matern(dot(jnp.concatenate(parts, axis=0), right, NN))
             stacked = [
-                tiles[64 * s:64 * s + 64, 128 * h:128 * h + 128] for s in range(len(rows)) for h in range(2)
+                tiles[64 * s:64 * s + 64, 128 * h:128 * h + 128] for s in range(len(sources)) for h in range(2)
             ]
             out = dot(jnp.concatenate(sides, axis=1), jnp.concatenate(stacked, axis=0), NN)
             last = jnp.sum(out[16:24], axis=0, keepdims=True)
-            put(i, jnp.concatenate([out[:16], jnp.broadcast_to(last, (8, 128))], axis=0))
+            out = jnp.concatenate([out[:16], jnp.broadcast_to(last, (8, 128))], axis=0)
+            if add:
+                acc[base + i] += out
+            else:
+                acc[base + i] = out
 
         def body(turn, carry):
             for at, entries in inside.items():
                 @pl.when(turn == at)
                 def _():
                     run(entries)
-            one(2 * turn)
-            one(2 * turn + 1)
+            for step in range(unroll):
+                one(unroll * turn + step)
             return carry
 
-        lax.fori_loop(0, HALF // 2, body, 0)
-
-    def put_own(base, first):
-        def put(i, out):
-            if first:
-                acc[base + i] = out
-            else:
-                acc[base + i] += out
-        return put
-
-    def put_part(dy):
-        def put(i, out):
-            part_out[dy - 1, i] = out
-        return put
-
-    def of_group(g):
-        return [(bufs[g], at) for at in range(2 * len(SOURCE_GROUPS[g]))]
-
-    def rows_of(g):
-        return [source_row(dx, dk) for dx in SOURCE_GROUPS[g] for dk in range(2)]
+        lax.fori_loop(0, outputs * HALF // unroll, body, 0)
+
+    def of_groups(*which):
+        sources = [(bufs[g], at) for g in which for at in range(2 * len(SOURCE_GROUPS[g]))]
+        rows = [source_row(dx, dk) for g in which for dx in SOURCE_GROUPS[g] for dk in range(2)]
+        return sources, rows
 
     for row in range(8):
         qall[row:row + 1, :] = jnp.zeros((1, 128), jnp.int32)
@@ -355,41 +343,57 @@
     to_smem.start()
     to_smem.wait()
     run([("s0", "")])
-    group(of_group(0), 0, first_smem, rows_of(0), put_own(0, True), {})
-
-    for kind in ("x", "y", "z"):
+    sources, rows = of_groups(0)
+    group(sources, first_smem, rows, 0, 1, False, 8, {})
+    run([("", "x2 y2")])
+
+    for kind in ("x", "y"):
         table(kind, "wait_recv")
     for row in range(8):
         qall[row:row + 1, :] = qrow[row, pl.ds(spot, 1), :]
-    for dy in range(4):
-        ptab[8 * dy:8 * dy + 8, :] = pairs(dy)
-    for row in range(8):
-        qall[row:row + 1, :] = zrow[row, pl.ds(z, 1), :]
-    ptab[N_COL:, :] = jnp.maximum(mine_ref[N_COL:, :], qall[...])
+    for k, dy in enumerate(OUTPUTS):
+        ptab[8 * k:8 * k + 8, :] = pairs(dy)
     to_smem = pltpu.make_async_copy(ptab, ptab_smem, local_sem.at[0])
     to_smem.start()
     to_smem.wait()
+    weigh(STACK)
 
     run([("x1", "s1"), ("x3", "s3")] + Z1 + [("s1 s3", "")])
-    group(of_group(1), 0, ptab_smem, rows_of(1), put_own(0, False), {3: [("x2", "s2")]})
-    run([("s2", "")])
-    group(of_group(2), 0, ptab_smem, rows_of(2), put_own(0, False), {1: Z2})
-    everything = of_group(0) + of_group(1) + of_group(2)
-    all_rows = rows_of(0) + rows_of(1) + rows_of(2)
-    for dy, inside in ((1, {}), (3, {0: Z3}), (2, {})):
-        run([("y%d" % dy, "")])
-        weigh(dy)
-        group(everything, 8 * dy, ptab_smem, [8 * dy + row for row in all_rows], put_part(dy), inside)
-        run([("", "r%d" % dy)])
+    sources, rows = of_groups(1)
+    group(sources, ptab_smem, rows, 0, 1, True, 4, {})
+
+    table("z", "wait_recv")
+    for row in range(8):
+        qall[row:row + 1, :] = zrow[row, pl.ds(z, 1), :]
+    last_tab[...] = jnp.maximum(mine_ref[N_COL:, :], qall[...])
+    to_smem = pltpu.make_async_copy(last_tab, last_smem, local_sem.at[1])
+    to_smem.start()
+
+    run([("y1 y3", "")])
+    weigh(1)
+    weigh(2)
+    sources, rows = of_groups(0, 1)
+    group(sources, ptab_smem, rows, HALF, 2, False, 4, {1: [("x2", "s2")], 2: Z2})
+    run([("s2 y2", "")])
+    weigh(3)
+    sources, rows = of_groups(2)
+    last_sources, last_rows = sources, rows
+    group(sources, ptab_smem, rows, HALF, 2, True, 8, {})
+    run([("", "r1 r3")] + Z3)
+    sources, rows = of_groups(0, 1, 2)
+    group(sources, ptab_smem, rows, 3 * HALF, 1, False, 4, {})
+    run([("", "r2")])
+    group(last_sources, ptab_smem, last_rows, 0, 1, True, 8, {})
     run([("u4a d4b", "")])
-    stack_rows = [N_COL + (z + N_ROW - d) % N_ROW for d in range(N_ROW)]
-    group([(bufz, d) for d in range(N_ROW)], 4 * HALF, ptab_smem, stack_rows, put_own(HALF, True), {})
+    to_smem.wait()
+    stack_rows = [(z + N_ROW - d) % N_ROW for d in range(N_ROW)]
+    group([(bufz, d) for d in range(N_ROW)], last_smem, stack_rows, STACK * HALF, 1, False, 4, {})
     run([("r1 r3 r2", "")])
 
     old = jnp.zeros((NV, 128), jnp.float32)
     curve = jnp.zeros((NV, 128), jnp.float32)
     for b in range(2 * HALF):
-        product = acc[b]
+        product = acc[b if b < HALF else STACK * HALF + b - HALF]
         if b < HALF:
             product = product + part_in[0, b] + part_in[1, b] + part_in[2, b]
         sides = sides_ref[:, b * BLK:(b + 1) * BLK]
@@ -432,26 +436,26 @@
 
     stat_out[...] = mine_stats
     stat1[c] = mine_stats
-    share(lambda at: stat_out, stat1, st_ssem, st_rsem, True, None, "start")
-    share(lambda at: stat_out, stat1, st_ssem, st_rsem, True, None, "wait_recv")
+    share(stat_out, stat1, True, "start")
+    for name in PLAN.events:
+        copy(name).wait_send()
+    for kind in KINDS:
+        table(kind, "wait_send")
+    share(stat_out, stat1, True, "wait_recv")
     old, curve, q, ratio, centre, moved = merge(stat1[...])
     n, d = moved(centre)
     row_stats = jnp.concatenate([old, curve, n, d, q, centre, old, old], axis=0)
     stat2_out[...] = row_stats
     stat2[z] = row_stats
-    share(lambda at: stat2_out, stat2, st_ssem, st_rsem, False, 0, "start")
-    share(lambda at: stat2_out, stat2, st_ssem, st_rsem, False, 0, "wait_recv")
+    share(stat2_out, stat2, False, "start")
+    share(stat_out, stat1, True, "wait_send")
+    share(stat2_out, stat2, False, "wait_recv")
     old, curve, q, ratio, centre, moved = merge(stat2[...])
     n, d = moved(ratio)
     pair = jnp.concatenate([ratio, n / old, jnp.zeros((126, 128), jnp.float32)], axis=0)
     coef_ref[...] = pair.T[0:24]
 
-    for name in PLAN.events:
-        copy(name).wait_send()
-    for kind in KINDS:
-        table(kind, "wait_send")
-    share(lambda at: stat_out, stat1, st_ssem, st_rsem, True, None, "wait_send")
-    share(lambda at: stat2_out, stat2, st_ssem, st_rsem, False, 0, "wait_send")
+    share(stat2_out, stat2, False, "wait_send")
 
 
 def iterate(states, right_sides, row_blocks, col_blocks, tile_counts):
@@ -465,9 +469,11 @@
             jax.ShapeDtypeStruct((NV, 2048), jnp.float32),
             jax.ShapeDtypeStruct((24, 128), jnp.float32),
         ),
-        in_specs=[pl.BlockSpec(memory_space=pltpu.SMEM), vmem, vmem, hbm, hbm],
+        in_specs=[pl.BlockSpec(memory_space=pltpu.SMEM), hbm, hbm, hbm, hbm],
         out_specs=(vmem, vmem),
         scratch_shapes=[
+            pltpu.VMEM((1, MAXT), jnp.int32),
+            pltpu.VMEM((1, MAXT), jnp.int32),
             pltpu.VMEM((FEAT, 2048), jnp.bfloat16),
             pltpu.VMEM((NV, 2048), jnp.float32),
         ] + [pltpu.VMEM((n, ROWS, 16, 128), jnp.bfloat16) for n in sizes] + [
@@ -475,8 +481,7 @@
             pltpu.VMEM((5 * HALF, 256, 256), jnp.bfloat16),
             pltpu.VMEM((HALF + 1, 16, 128), jnp.bfloat16),
             pltpu.VMEM((HALF + 1, 32, 128), jnp.bfloat16),
-            pltpu.VMEM((2 * HALF, 24, 128), jnp.float32),
-            pltpu.VMEM((3, HALF, 24, 128), jnp.float32),
+            pltpu.VMEM((5 * HALF, 24, 128), jnp.float32),
             pltpu.VMEM((3, HALF, 24, 128), jnp.float32),
             pltpu.VMEM((40, 128), jnp.int32),
             table,
@@ -485,8 +490,10 @@
             pltpu.VMEM((8, 8, 128), jnp.int32),
             pltpu.VMEM((8, 8, 128), jnp.int32),
             table,
-            pltpu.VMEM((40, 128), jnp.int32),
-            pltpu.SMEM((40, 128), jnp.int32),
+            pltpu.VMEM((N_COL, 128), jnp.int32),
+            pltpu.SMEM((N_COL, 128), jnp.int32),
+            table,
+            pltpu.SMEM((8, 128), jnp.int32),
             table,
             pltpu.SMEM((8, 128), jnp.int32),
             pltpu.VMEM((8, 128), jnp.float32),
@@ -499,10 +506,10 @@
             pltpu.SemaphoreType.DMA((N_COL + N_ROW,)),
             pltpu.SemaphoreType.DMA((N_COL + N_ROW,)),
             pltpu.SemaphoreType.DMA((N_COL + N_ROW,)),
-            pltpu.SemaphoreType.DMA((2,)),
+            pltpu.SemaphoreType.DMA((4,)),
         ],
         compiler_params=pltpu.CompilerParams(
-            collective_id=0, has_side_effects=True, vmem_limit_bytes=40 * 1024 * 1024
+            collective_id=0, has_side_effects=True, vmem_limit_bytes=60 * 1024 * 1024
         ),
         name="gather_apply_reduce",
     )(tile_counts, row_blocks, col_blocks, states.T, right_sides)

time: 57.9 us -> 53.6 us (0.926)
  Pallas kernels: 53.4 us -> 49.2 us
  local copies, waits for them, and re-layouts: 2.05 us -> 0.97 us
  other arithmetic: 0.92 us -> 1.84 us
    pallas_call x1, Pallas kernels: 53.4 us -> 49.2 us  [iterate(): pl.pallas_call(kernel, out_shape=(jax.ShapeDtypeStruct((NV, 2048), jnp.fl...]
    unnamed x8 -> x2, local copies, waits for them, and re-layouts: 1.88 us -> 0.01 us
    add x1, other arithmetic: 0.92 us -> 1.84 us  [shards(): return (step_size * right_sides, residual, residual + ratio * right_sides)]
    slice x1, local copies, waits for them, and re-layouts: 0.17 us -> 0.96 us  [shards(): step_size, ratio = (coef[:NV, 0:1], coef[:NV, 1:2])]
where the time goes in v2:
time: 53.6 us; the launch traced here: 53.3 us
  Pallas kernels  49.2 us (92%)
  other arithmetic  1.84 us (3%)
  between operations  1.3 us (2%)
  local copies, waits for them, and re-layouts  0.97 us (2%)
    pallas_call x1, Pallas kernels, iterate(): pl.pallas_call(kernel, out_shape=(jax.ShapeDtypeStruct((NV, 2048), jnp.fl...  49.2 us
    add x1, other arithmetic, shards(): return (step_size * right_sides, residual, residual + ratio * right_sides)  1.84 us

profile of v2, /device:TPU:1, one launch (start us, length us, event | category | flops | bytes accessed | tf_op | source)
XLA Modules:
  0.0 53.3 jit_solution(3325731515651300)
XLA Ops:
  1.3 0.0 copy-start
  1.3 49.2 %gather_apply_reduce.1 = (f32[17,2048]{1,0:T(8,128)}, f32[24,128]{1,0:T(8,128)}) custom-call(s32[1]{0:T(128)S(6)} %copy.8.count_ref, s32[1,320]{1,0:T(1,128)} %u_hbm.1, s32[1,320]{1,0:T(1,128)} %v_hbm.1, bf16[64,2048]{1,0:T(8,128)(2,1)} %bitcast.1, f32[17,2048]{1,0:T(8,128)} %sides_hbm.1), custom_call_target="tpu_custom_call" | custom-call | tf_op jit(solution)/shard_map/gather_apply_reduce/pallas_call | solution.py:466
  50.5 1.0 %slice_reduce_fusion = (f32[17]{0:T(128)S(1)}, f32[17]{0:T(128)S(1)}) fusion(f32[24,128]{1,0:T(8,128)} %get-tuple-element.5), kind=kLoop, calls=%fused_computation.3 | loop fusion | bytes 272 | tf_op jit(solution)/shard_map/slice | solution.py:520
  51.5 0.0 copy-done
  51.5 1.8 %multiply_add_fusion = (f32[17,2048]{1,0:T(8,128)}, f32[17,2048]{1,0:T(8,128)}, f32[17,2048]{1,0:T(8,128)}) fusion(f32[17,2048]{1,0:T(8,128)S(1)} %copy-done, f32[17]{0:T(128)S(1)} %get-tuple-element.7, f32[17,2048]{1,0:T(8,128)} %get-tuple-element.6, f32[17]{0:T(128)S(1)} %get-tuple-element.8), kind=kLoop, calls=%fused_computation | loop fusion | flops 174080 | bytes 696456 | tf_op jit(solution)/shard_map/add | solution.py:522
Async XLA Ops:
  1.3 50.2 %copy-start = (f32[17,2048]{1,0:T(8,128)S(1)}, f32[17,2048]{1,0:T(8,128)}, u32[]{:S(2)}) copy-start(f32[17,2048]{1,0:T(8,128)} %sides_hbm.1) | copy-start | bytes 417796

commit v3 on v2

--- a/solution.py
+++ b/solution.py
@@ -44,10 +44,10 @@
     return high, middle, rest - middle
 
 
-SOURCE_GROUPS = ((0,), (1, 3), (2,))
+SOURCE_GROUPS = (((0, 0), (0, 1)), ((1, 0), (3, 0)), ((1, 1), (3, 1)), ((2, 0), (2, 1)))
+PLACE = {slot: (g, at) for g, group in enumerate(SOURCE_GROUPS) for at, slot in enumerate(group)}
 OUTPUTS = (0, 1, 3, 2)
 STACK = 4
-PLACE = {dx: (g, 2 * k) for g, group in enumerate(SOURCE_GROUPS) for k, dx in enumerate(group)}
 
 
 class Plan:
@@ -57,14 +57,14 @@
             self.add("x%d" % m, "source", 0, (0, ROWS), m)
             self.add("y%d" % m, "output", 0, None, m)
             self.add("r%d" % m, "return", m, None, m)
-        for dx in PLACE:
+        for dx in range(4):
             self.add("s%d" % dx, "sibling", dx, (0, ROWS), 0)
-        for step in range(4):
-            for part, rows in (("a", PART_A), ("b", PART_B)):
-                if step < 3 or part == "a":
-                    self.add("u%d%s" % (step + 1, part), "stack", step, rows, 1)
-                if step < 3 or part == "b":
-                    self.add("d%d%s" % (step + 1, part), "stack", (8 - step) % 8, rows, 7)
+        for part, rows in (("a", PART_A), ("b", PART_B)):
+            for step in range(3):
+                self.add("u%d%s" % (step + 1, part), "stack", step, rows, 1)
+                self.add("d%d%s" % (step + 1, part), "stack", (8 - step) % 8, rows, 7)
+        self.add("u4a", "stack", 2, PART_A, 2)
+        self.add("d4b", "stack", 6, PART_B, 6)
 
     def add(self, name, *what):
         self.events[name] = (len(self.events),) + what
@@ -80,14 +80,14 @@
 
 ROUND0 = names("s0 x1 x3 y1") + names("y3 u1a d1a") + names("u1b d1b")
 Z1 = [("u1a", "u2a"), ("d1a", "d2a"), ("u1b", "u2b"), ("d1b", "d2b")]
-Z2 = [("u2a", "u3a"), ("d2a", "d3a"), ("u2b", "u3b"), ("d2b", "d3b")]
-Z3 = [("u3a", "u4a"), ("d3b", "d4b"), ("u3b d3a", "")]
+Z2A = [("u2a", "u3a u4a"), ("d2a", "d3a")]
+Z2B = [("d2b", "d4b d3b"), ("u2b", "u3b")]
 
 
 def kernel(
     count_ref, u_hbm, v_hbm, states_hbm, sides_hbm,
-    applied_ref, coef_ref,
-    u_ref, v_ref, states_ref, sides_ref, buf0, buf1, buf2, bufz, turned_ref, weights, mask_e, mask_v, acc, part_in,
+    applied_hbm, coef_ref,
+    applied_ref, u_ref, v_ref, states_ref, sides_ref, buf0, buf1, buf2, buf3, bufz, turned_ref, weights, mask_e, mask_v, acc, part_in,
     mine_ref, theirs_ref, wide_ref, prow, qrow, zrow, qall, ptab, ptab_smem, first_tab, first_smem, last_tab, last_smem,
     stat_out, stat1, stat2, stat2_out,
     ssem, rsem, tab_ssem, tab_rsem, st_ssem, st_rsem, local_sem,
@@ -95,7 +95,7 @@
     z = lax.axis_index("row")
     c = lax.axis_index("col")
     cy, cx, ck = c // 8, (c // 2) % 4, c % 2
-    bufs = (buf0, buf1, buf2)
+    bufs = (buf0, buf1, buf2, buf3)
     spot = 2 * cx + ck
     load_states = pltpu.make_async_copy(states_hbm, states_ref, local_sem.at[0])
     load_sides = pltpu.make_async_copy(sides_hbm, sides_ref, local_sem.at[1])
@@ -132,13 +132,14 @@
             target = ((z + move) % N_ROW, c)
         elif kind == "source":
             src = buf0.at[0, span]
-            to_g, to_at = PLACE[move]
+            to_g, to_at = PLACE[move, 0]
             dst = bufs[to_g].at[to_at, span]
             target = (z, col_of(move, 0, 0))
         elif kind == "sibling":
-            g, at = PLACE[slot]
+            g, at = PLACE[slot, 0]
+            to_g, to_at = PLACE[slot, 1]
             src = bufs[g].at[at, span]
-            dst = bufs[g].at[at + 1, span]
+            dst = bufs[to_g].at[to_at, span]
             target = (z, col_of(0, 0, 1))
         elif kind == "output":
             src = turned_ref.at[0]
@@ -328,8 +329,8 @@
         lax.fori_loop(0, outputs * HALF // unroll, body, 0)
 
     def of_groups(*which):
-        sources = [(bufs[g], at) for g in which for at in range(2 * len(SOURCE_GROUPS[g]))]
-        rows = [source_row(dx, dk) for g in which for dx in SOURCE_GROUPS[g] for dk in range(2)]
+        sources = [(bufs[g], at) for g in which for at in range(2)]
+        rows = [source_row(dx, dk) for g in which for dx, dk in SOURCE_GROUPS[g]]
         return sources, rows
 
     for row in range(8):
@@ -358,9 +359,10 @@
     to_smem.wait()
     weigh(STACK)
 
-    run([("x1", "s1"), ("x3", "s3")] + Z1 + [("s1 s3", "")])
+    run(Z1)
+    run([("x1", "s1"), ("x3", "s3")])
     sources, rows = of_groups(1)
-    group(sources, ptab_smem, rows, 0, 1, True, 4, {})
+    group(sources, ptab_smem, rows, 0, 1, True, 8, {})
 
     table("z", "wait_recv")
     for row in range(8):
@@ -369,22 +371,27 @@
     to_smem = pltpu.make_async_copy(last_tab, last_smem, local_sem.at[1])
     to_smem.start()
 
-    run([("y1 y3", "")])
+    run([("y1", "")])
     weigh(1)
-    weigh(2)
-    sources, rows = of_groups(0, 1)
-    group(sources, ptab_smem, rows, HALF, 2, False, 4, {1: [("x2", "s2")], 2: Z2})
+    run([("s1 s3", "")])
+    sources, rows = of_groups(0, 1, 2)
+    group(sources, ptab_smem, rows, HALF, 1, False, 4, {1: Z2A + [("x2", "s2")]})
+    run(Z2B)
+    sources, rows = of_groups(2)
+    group(sources, ptab_smem, rows, 0, 1, True, 8, {})
     run([("s2 y2", "")])
     weigh(3)
-    sources, rows = of_groups(2)
-    last_sources, last_rows = sources, rows
-    group(sources, ptab_smem, rows, HALF, 2, True, 8, {})
-    run([("", "r1 r3")] + Z3)
-    sources, rows = of_groups(0, 1, 2)
+    sources, rows = of_groups(0, 1, 2, 3)
     group(sources, ptab_smem, rows, 3 * HALF, 1, False, 4, {})
-    run([("", "r2")])
+    last_sources, last_rows = of_groups(3)
+    run([("y3", "r2")])
+    group(last_sources, ptab_smem, last_rows, HALF, 1, True, 8, {})
+    run([("", "r1")])
+    weigh(2)
+    group(sources, ptab_smem, rows, 2 * HALF, 1, False, 4, {})
+    run([("", "r3")])
     group(last_sources, ptab_smem, last_rows, 0, 1, True, 8, {})
-    run([("u4a d4b", "")])
+    run([("u3a u3b u4a", ""), ("d3a d3b d4b", "")])
     to_smem.wait()
     stack_rows = [(z + N_ROW - d) % N_ROW for d in range(N_ROW)]
     group([(bufz, d) for d in range(N_ROW)], last_smem, stack_rows, STACK * HALF, 1, False, 4, {})
@@ -401,6 +408,8 @@
         applied_ref[:, b * BLK:(b + 1) * BLK] = applied
         old += sides * sides
         curve += sides * applied
+    save = pltpu.make_async_copy(applied_ref, applied_hbm, local_sem.at[0])
+    save.start()
     old = jnp.sum(old, axis=1, keepdims=True)
     curve = jnp.sum(curve, axis=1, keepdims=True)
     centre = jnp.where(curve > 0.0, jnp.minimum(old / curve, 1.0), 1.0)
@@ -454,6 +463,7 @@
     n, d = moved(ratio)
     pair = jnp.concatenate([ratio, n / old, jnp.zeros((126, 128), jnp.float32)], axis=0)
     coef_ref[...] = pair.T[0:24]
+    save.wait()
 
     share(stat2_out, stat2, False, "wait_send")
 
@@ -461,7 +471,7 @@
 def iterate(states, right_sides, row_blocks, col_blocks, tile_counts):
     vmem = pl.BlockSpec(memory_space=pltpu.VMEM)
     hbm = pl.BlockSpec(memory_space=pltpu.HBM)
-    sizes = [2 * len(group) for group in SOURCE_GROUPS] + [N_ROW]
+    sizes = [len(group) for group in SOURCE_GROUPS] + [N_ROW]
     table = pltpu.VMEM((8, 128), jnp.int32)
     return pl.pallas_call(
         kernel,
@@ -470,8 +480,9 @@
             jax.ShapeDtypeStruct((24, 128), jnp.float32),
         ),
         in_specs=[pl.BlockSpec(memory_space=pltpu.SMEM), hbm, hbm, hbm, hbm],
-        out_specs=(vmem, vmem),
+        out_specs=(hbm, vmem),
         scratch_shapes=[
+            pltpu.VMEM((NV, 2048), jnp.float32),
             pltpu.VMEM((1, MAXT), jnp.int32),
             pltpu.VMEM((1, MAXT), jnp.int32),
             pltpu.VMEM((FEAT, 2048), jnp.bfloat16),

time: 53.6 us -> 51.9 us (0.968)
  Pallas kernels: 49.2 us -> 47.5 us
    pallas_call x1, Pallas kernels: 49.2 us -> 47.5 us  [iterate(): pl.pallas_call(kernel, out_shape=(jax.ShapeDtypeStruct((NV, 2048), jnp.fl...]
where the time goes in v3:
time: 51.9 us; the launch traced here: 51.6 us
  Pallas kernels  47.5 us (92%)
  other arithmetic  1.84 us (4%)
  between operations  1.3 us (3%)
  local copies, waits for them, and re-layouts  0.97 us (2%)
    pallas_call x1, Pallas kernels, iterate(): pl.pallas_call(kernel, out_shape=(jax.ShapeDtypeStruct((NV, 2048), jnp.fl...  47.5 us
    add x1, other arithmetic, shards(): return (step_size * right_sides, residual, residual + ratio * right_sides)  1.84 us

profile of v3, /device:TPU:1, one launch (start us, length us, event | category | flops | bytes accessed | tf_op | source)
XLA Modules:
  0.0 51.6 jit_solution(2168320449694121430)
XLA Ops:
  1.3 0.0 copy-start
  1.3 47.5 %gather_apply_reduce.1 = (f32[17,2048]{1,0:T(8,128)}, f32[24,128]{1,0:T(8,128)}) custom-call(s32[1]{0:T(128)S(6)} %copy.8.count_ref, s32[1,320]{1,0:T(1,128)} %u_hbm.1, s32[1,320]{1,0:T(1,128)} %v_hbm.1, bf16[64,2048]{1,0:T(8,128)(2,1)} %bitcast.1, f32[17,2048]{1,0:T(8,128)} %sides_hbm.1), custom_call_target="tpu_custom_call" | custom-call | tf_op jit(solution)/shard_map/gather_apply_reduce/pallas_call | solution.py:476
  48.8 1.0 %slice_reduce_fusion = (f32[17]{0:T(128)S(1)}, f32[17]{0:T(128)S(1)}) fusion(f32[24,128]{1,0:T(8,128)} %get-tuple-element.5), kind=kLoop, calls=%fused_computation.3 | loop fusion | bytes 272 | tf_op jit(solution)/shard_map/slice | solution.py:531
  49.8 0.0 copy-done
  49.8 1.8 %multiply_add_fusion = (f32[17,2048]{1,0:T(8,128)}, f32[17,2048]{1,0:T(8,128)}, f32[17,2048]{1,0:T(8,128)}) fusion(f32[17,2048]{1,0:T(8,128)S(1)} %copy-done, f32[17]{0:T(128)S(1)} %get-tuple-element.7, f32[17,2048]{1,0:T(8,128)} %get-tuple-element.6, f32[17]{0:T(128)S(1)} %get-tuple-element.8), kind=kLoop, calls=%fused_computation | loop fusion | flops 174080 | bytes 696456 | tf_op jit(solution)/shard_map/add | solution.py:533
Async XLA Ops:
  1.3 48.5 %copy-start = (f32[17,2048]{1,0:T(8,128)S(1)}, f32[17,2048]{1,0:T(8,128)}, u32[]{:S(2)}) copy-start(f32[17,2048]{1,0:T(8,128)} %sides_hbm.1) | copy-start | bytes 417796

commit v4 on v3

--- a/solution.py
+++ b/solution.py
@@ -281,10 +281,14 @@
                 device_id=(z, col_of(mx, my, mk)), device_id_type=MESH), method)()
 
     KINDS = ("sibling", "x", "y", "z")
-    for kind in KINDS:
+    for kind in ("sibling", "x"):
         table(kind, "start")
-    for name in ROUND0:
+    for name in ROUND0[:3]:
         copy(name).start()
+    table("y", "start")
+    for name in ROUND0[3:]:
+        copy(name).start()
+    table("z", "start")
 
     def pairs(dy):
         shift = (128 - 8 * ((cy + 4 - dy) % 4)) % 128

time: 51.9 us -> 51.9 us (level)
  no operation moved by 1% of the time
where the time goes in v4:
time: 51.9 us; the launch traced here: 51.6 us
  Pallas kernels  47.5 us (92%)
  other arithmetic  1.84 us (4%)
  between operations  1.3 us (3%)
  local copies, waits for them, and re-layouts  0.97 us (2%)
    pallas_call x1, Pallas kernels, iterate(): pl.pallas_call(kernel, out_shape=(jax.ShapeDtypeStruct((NV, 2048), jnp.fl...  47.5 us
    add x1, other arithmetic, shards(): return (step_size * right_sides, residual, residual + ratio * right_sides)  1.84 us

profile of v4, /device:TPU:1, one launch (start us, length us, event | category | flops | bytes accessed | tf_op | source)
XLA Modules:
  0.0 51.6 jit_solution(13779565132220773728)
XLA Ops:
  1.3 0.0 copy-start
  1.3 47.5 %gather_apply_reduce.1 = (f32[17,2048]{1,0:T(8,128)}, f32[24,128]{1,0:T(8,128)}) custom-call(s32[1]{0:T(128)S(6)} %copy.8.count_ref, s32[1,320]{1,0:T(1,128)} %u_hbm.1, s32[1,320]{1,0:T(1,128)} %v_hbm.1, bf16[64,2048]{1,0:T(8,128)(2,1)} %bitcast.1, f32[17,2048]{1,0:T(8,128)} %sides_hbm.1), custom_call_target="tpu_custom_call" | custom-call | tf_op jit(solution)/shard_map/gather_apply_reduce/pallas_call | solution.py:480
  48.8 1.0 %slice_reduce_fusion = (f32[17]{0:T(128)S(1)}, f32[17]{0:T(128)S(1)}) fusion(f32[24,128]{1,0:T(8,128)} %get-tuple-element.5), kind=kLoop, calls=%fused_computation.3 | loop fusion | bytes 272 | tf_op jit(solution)/shard_map/slice | solution.py:535
  49.8 0.0 copy-done
  49.8 1.8 %multiply_add_fusion = (f32[17,2048]{1,0:T(8,128)}, f32[17,2048]{1,0:T(8,128)}, f32[17,2048]{1,0:T(8,128)}) fusion(f32[17,2048]{1,0:T(8,128)S(1)} %copy-done, f32[17]{0:T(128)S(1)} %get-tuple-element.7, f32[17,2048]{1,0:T(8,128)} %get-tuple-element.6, f32[17]{0:T(128)S(1)} %get-tuple-element.8), kind=kLoop, calls=%fused_computation | loop fusion | flops 174080 | bytes 696456 | tf_op jit(solution)/shard_map/add | solution.py:537
Async XLA Ops:
  1.3 48.5 %copy-start = (f32[17,2048]{1,0:T(8,128)S(1)}, f32[17,2048]{1,0:T(8,128)}, u32[]{:S(2)}) copy-start(f32[17,2048]{1,0:T(8,128)} %sides_hbm.1) | copy-start | bytes 417796
